TPU v7x, 512 devices: a whole 4x4x16 slice. The times are simulated.
512 devices in a mesh: dp: 2 (over core), fsdp: 32 (over y, z_lo), tensor: 8 (over z_hi, x).
Axes of the slice: x: 4, y: 4, z: 16 (z_hi: 2, z_lo: 8; z = z_hi * 8 + z_lo), core: 2. Of those that a mesh axis runs over, the one named last changes fastest.
Arguments:
- tokens: bfloat16 [16384, 4096], P(('dp', 'fsdp', 'tensor')), may hold values from -40 to 40
- norm_gain: float32 [4096], replicated, may hold values from 0.5 to 1.5
- tile_values: bfloat16 [512, 128, 128], P(('fsdp', 'tensor')), may hold values from -0.25 to 0.25
- tile_rows: int32 [8, 64], P('tensor'), may hold values from 0 to 31, as said below
- tile_cols: int32 [8, 64], P('tensor'), may hold values from 0 to 13
- tile_counts: int32 [8, 32], P('tensor'), may hold values from 0 to 2, as said below
- grad_out: bfloat16 [16384, 14336], P(('dp', 'fsdp'), 'tensor'), may hold values from -3 to 3
Outputs:
- mixed: bfloat16 [16384, 14336], P(('dp', 'fsdp'), 'tensor')
- grad_x: bfloat16 [16384, 4096], P(('dp', 'fsdp', 'tensor'))
- grad_gain: float32 [4096], replicated
- grad_tiles: float32 [512, 128, 128], P(('fsdp', 'tensor'))
Inputs may be any that keep to these rules, and one draw needn't show every extreme that they name: `tile_counts`: for each tensor index the counts over the 32 fsdp shards sum to 56, and some shard holds exactly 2. `tile_rows`: within one tensor index the (row, column) pairs of held slots are all different.
All inputs are finite; a program needn't handle non-finite values.
Results may differ from a plain program's by a relative error of at most 0.013.
Values may be sent and summed in bfloat16 or wider, within the bound.
A program may use at most 128 MiB of HBM per device.

v0:
```python
import jax
import jax.numpy as jnp
from jax import lax
from jax.sharding import PartitionSpec as P


def tile_forward(group_rows, values, rows_list, cols_list, col_tiles):
    tile_size = values.shape[1]
    blocks = group_rows.reshape(group_rows.shape[0], -1, tile_size)
    picked = jnp.take(blocks, rows_list, axis=1)
    product = jnp.einsum("tsk,skn->tsn", picked, values, preferred_element_type=jnp.float32)
    placed = (
        jnp.zeros((group_rows.shape[0], col_tiles, tile_size), jnp.float32)
        .at[:, cols_list]
        .add(product)
    )
    return placed.reshape(group_rows.shape[0], col_tiles * tile_size)


def tile_backward(grad_rows, values, rows_list, cols_list, row_tiles):
    tile_size = values.shape[1]
    blocks = grad_rows.reshape(grad_rows.shape[0], -1, tile_size)
    picked = jnp.take(blocks, cols_list, axis=1)
    product = jnp.einsum("tsn,skn->tsk", picked, values, preferred_element_type=jnp.float32)
    placed = (
        jnp.zeros((grad_rows.shape[0], row_tiles, tile_size), jnp.float32)
        .at[:, rows_list]
        .add(product)
    )
    return placed.reshape(grad_rows.shape[0], row_tiles * tile_size)


def per_device(tokens, norm_gain, tile_values, tile_rows, tile_cols, tile_counts, grad_out):
    tile_size = tile_values.shape[1]
    slot_cap = tile_values.shape[0]
    row_tiles = tokens.shape[1] // tile_size
    col_tiles = grad_out.shape[1] // tile_size
    rows_list = tile_rows[0]
    cols_list = tile_cols[0]
    shard_counts = tile_counts[0]
    held_all = (jnp.arange(slot_cap)[None, :] < shard_counts[:, None]).reshape(-1)
    own_held = jnp.arange(slot_cap) < shard_counts[lax.axis_index("fsdp")]
    local_float = tokens.astype(jnp.float32)
    inv_rms = lax.rsqrt(jnp.mean(local_float * local_float, axis=1, keepdims=True) + 1e-05)
    scaled = local_float * inv_rms
    normed = (scaled * norm_gain).astype(jnp.bfloat16)
    group_rows = lax.all_gather(normed, "tensor", axis=0, tiled=True)
    gathered = lax.all_gather(tile_values, "fsdp", axis=0, tiled=True)
    kept_values = jnp.where(held_all[:, None, None], gathered, jnp.zeros_like(gathered))
    outputs = tile_forward(group_rows, kept_values, rows_list, cols_list, col_tiles)
    mixed = outputs.astype(jnp.bfloat16)
    input_grad = lax.psum_scatter(
        tile_backward(grad_out, kept_values, rows_list, cols_list, row_tiles).astype(jnp.bfloat16),
        "tensor",
        scatter_dimension=0,
        tiled=True,
    ).astype(jnp.float32)
    x_blocks = group_rows.reshape(group_rows.shape[0], row_tiles, tile_size)
    g_blocks = grad_out.reshape(grad_out.shape[0], col_tiles, tile_size)
    picked_x = jnp.take(x_blocks, rows_list, axis=1)
    picked_g = jnp.take(g_blocks, cols_list, axis=1)
    grad_shard = lax.psum_scatter(
        jnp.einsum("tsk,tsn->skn", picked_x, picked_g, preferred_element_type=jnp.float32),
        "fsdp",
        scatter_dimension=0,
        tiled=True,
    )
    grad_shard = jnp.where(own_held[:, None, None], grad_shard, jnp.zeros_like(grad_shard))
    grad_tiles = lax.psum(grad_shard, "dp")
    gain_part = jnp.sum(input_grad * scaled, axis=0)
    grad_gain = lax.psum(gain_part, ("dp", "fsdp", "tensor"))
    hidden_grad = input_grad * norm_gain
    grad_x = (
        inv_rms * (hidden_grad - scaled * jnp.mean(hidden_grad * scaled, axis=1, keepdims=True))
    ).astype(jnp.bfloat16)
    return (mixed, grad_x, grad_gain, grad_tiles)


def solution(mesh):
    placed = (
        P(("dp", "fsdp", "tensor"), None),
        P(),
        P(("fsdp", "tensor"), None, None),
        P("tensor", None),
        P("tensor", None),
        P("tensor", None),
        P(("dp", "fsdp"), "tensor"),
    )
    return jax.shard_map(
        per_device,
        mesh=mesh,
        in_specs=placed,
        out_specs=(
            P(("dp", "fsdp"), "tensor"),
            P(("dp", "fsdp", "tensor"), None),
            P(),
            P(("fsdp", "tensor"), None, None),
        ),
        check_vma=False,
    )
```

profile of v0, /device:TPU:1, one launch (start us, length us, event | category | flops | bytes accessed | tf_op | source)
XLA Modules:
  0.0 848.5 jit_solution(9026113694259479338)
XLA Ops:
  7.9 1.5 copy.32
  11.6 3.1 gather_fusion.1
  14.7 207.7 %all-gather.3.cloned.1.call-done = bf16[64,128,128]{2,1,0:T(8,128)(2,1)} async-done(((bf16[2,128,128]{2,1,0:T(8,128)(2,1)}), bf16[64,128,128]{2,1,0:T(8,128)(2,1)}) %all-gather.3.cloned.1.call-update) | async-done | bytes 2097168 | tf_op jit(solution)/shard_map/all_gather | solution.py:48
  222.3 7.4 fusion.2
  229.8 2.4 broadcast_in_dim.57
  232.2 19.4 %scatter_fusion.1 = f32[256,32,128]{2,0,1:T(8,128)} fusion(f32[256,32,128]{2,0,1:T(8,128)} %broadcast_in_dim.57, s32[64]{0:T(128)S(1)} %fusion.18, f32[64,256,128]{2,1,0:T(8,128)} %fusion.2), kind=kCustom, calls=%fused_computation.3 | custom fusion | flops 2097152 | bytes 25166080 | tf_op jit(solution)/shard_map/scatter-add | solution.py:28
  251.6 2.5 convert_element_type.28
  254.1 2.9 copy.34
  257.0 4.1 copy.39
  261.4 162.8 %reduce-scatter.7.cloned.1.call-done = bf16[32,4096]{1,0:T(8,128)(2,1)} async-done(((bf16[256,4096]{1,0:T(8,128)(2,1)}), bf16[32,4096]{1,0:T(8,128)(2,1)}) %reduce-scatter.7.cloned.1.call-update) | async-done | bytes 262160 | tf_op jit(solution)/shard_map/reduce_scatter | solution.py:52
  425.5 1.9 fusion.12
  427.6 109.9 %all-gather.5.cloned.1.call-done = bf16[256,4096]{1,0:T(8,128)(2,1)} async-done(((bf16[32,4096]{1,0:T(8,128)(2,1)}), bf16[256,4096]{1,0:T(8,128)(2,1)}) %all-gather.5.cloned.1.call-update) | async-done | bytes 2097168 | tf_op jit(solution)/shard_map/all_gather | solution.py:47
  537.5 4.1 copy.29
  541.6 3.2 copy.30
  544.8 3.0 gather_fusion
  547.8 7.0 fusion
  556.7 103.2 %psum.14 = f32[4096]{0:T(1024)} all-reduce(f32[4096]{0:T(1024)S(1)} %get-tuple-element.18), channel_id=1, replica_groups=mesh['dp'=2,'fsdp'=32,'tensor'=8] {'dp','fsdp','tensor'}, use_global_device_ids=true, to_apply=%region_6.9 | all-reduce | flops 4096 | bytes 32768 | tf_op jit(solution)/shard_map/psum | solution.py:71
  659.9 119.5 %reduce-scatter.5.cloned.1.call-done = f32[2,128,128]{2,1,0:T(8,128)} async-done(((f32[64,128,128]{2,1,0:T(8,128)}), f32[2,128,128]{2,1,0:T(8,128)}) %reduce-scatter.5.cloned.1.call-update) | async-done | bytes 131088 | tf_op jit(solution)/shard_map/reduce_scatter | solution.py:62
  779.5 1.6 broadcast_select_fusion.9
  781.1 6.7 fusion.5
  788.0 12.4 %scatter_fusion = f32[256,14,128]{2,0,1:T(8,128)S(1)} fusion(f32[256,14,128]{2,0,1:T(8,128)S(1)} %broadcast_in_dim.54, s32[64]{0:T(128)S(1)} %fusion.17, f32[64,256,128]{2,1,0:T(8,128)} %fusion.5), kind=kCustom, calls=%fused_computation.2 | custom fusion | flops 2097152 | bytes 25166080 | tf_op jit(solution)/shard_map/scatter-add | solution.py:15
  801.2 1.4 copy.37
  802.5 37.8 %all-reduce.2.cloned.1.call-done = f32[2,128,128]{2,1,0:T(8,128)} async-done(((f32[2,128,128]{2,1,0:T(8,128)}), f32[2,128,128]{2,1,0:T(8,128)}) %all-reduce.2.cloned.1.call-update) | async-done | bytes 131088 | tf_op jit(solution)/shard_map/psum | solution.py:69
  840.4 1.6 copy.44
  (41 shorter events, 7.2 us)
Async XLA Ops:
  7.2 215.2 %all-gather.3.cloned.1.call-start = ((), (), s32[]{:S(2)}) async-start(), calls=%async_computation.2 | async-start | bytes 2162688 | tf_op jit(solution)/shard_map/all_gather | solution.py:48
  7.9 416.4 %reduce-scatter.7.cloned.1.call-start = ((), (), s32[]{:S(2)}) async-start(), calls=%async_computation.6 | async-start | bytes 2359296 | tf_op jit(solution)/shard_map/reduce_scatter | solution.py:52
  11.6 3.1 copy-start.4
  11.6 3.1 copy-start.5
  257.0 4.2 copy-start.1
  257.0 167.2 %copy-start.2 = (f32[4096]{0:T(1024)S(1)}, f32[4096]{0:T(1024)}, u32[]{:S(2)}) copy-start(f32[4096]{0:T(1024)} %param.12) | copy-start | bytes 49156
  261.2 276.3 %all-gather.5.cloned.1.call-start = ((), (), s32[]{:S(2)}) async-start(), calls=%async_computation.3 | async-start | bytes 2359296 | tf_op jit(solution)/shard_map/all_gather | solution.py:47
  427.5 352.0 %reduce-scatter.5.cloned.1.call-start = ((), (), s32[]{:S(2)}) async-start(), calls=%async_computation.4 | async-start | bytes 4325376 | tf_op jit(solution)/shard_map/reduce_scatter | solution.py:62
  554.8 0.7 copy-start.3
  554.8 226.3 %copy-start = (bf16[64,128,128]{2,1,0:T(8,128)(2,1)S(1)}, bf16[64,128,128]{2,1,0:T(8,128)(2,1)}, u32[]{:S(2)}) copy-start(bf16[64,128,128]{2,1,0:T(8,128)(2,1)} %all-gather.3.cloned.1.call-done) | copy-start | bytes 6291460
  554.9 285.5 %all-reduce.2.cloned.1.call-start = ((), (), s32[]{:S(2)}) async-start(), calls=%async_computation.5 | async-start | bytes 262144 | tf_op jit(solution)/shard_map/psum | solution.py:69
Sparse Core Ops, SparseCore 0:
  10.1 212.2 all-gather.2
  261.3 162.8 reduce-scatter.6
  428.5 108.9 all-gather.4
  555.0 224.4 reduce-scatter.4
  783.0 57.3 all-reduce.1
where the time goes:
time: 849 us; the launch traced here: 848 us
  waiting for transfers between devices  639 us (75%)
  blocking collectives  103 us (12%)
  other arithmetic  41.6 us (5%)
  local copies, waits for them, and re-layouts  29.9 us (4%)
  matrix products  21.2 us (2%)
  between operations  13.9 us (2%)
    all_gather x1, waiting for transfers between devices, per_device(): gathered = lax.all_gather(tile_values, 'fsdp', axis=0, tiled=True)  208 us
    reduce_scatter x1, waiting for transfers between devices, per_device(): lax.psum_scatter(tile_backward(grad_out, kept_values, rows_list, cols_lis...  163 us
    reduce_scatter x1, waiting for transfers between devices, per_device(): lax.psum_scatter(jnp.einsum('tsk,tsn->skn', picked_x, picked_g, preferred...  120 us
    all_gather x1, waiting for transfers between devices, per_device(): group_rows = lax.all_gather(normed, 'tensor', axis=0, tiled=True)  110 us
    psum x1, blocking collectives, per_device(): grad_gain = lax.psum(gain_part, ('dp', 'fsdp', 'tensor'))  103 us
    psum x1, waiting for transfers between devices, per_device(): grad_tiles = lax.psum(grad_shard, 'dp')  37.8 us
    scatter-add x1, other arithmetic, tile_backward(): placed = jnp.zeros((grad_rows.shape[0], row_tiles, tile_size), jnp.float3...  19.4 us
  transfers between devices with their start and end apart: 5, of which 5 were waited for; matrix products, arithmetic and copies ran while one was open for 3% of the time, Pallas kernels for 0%

commit v1 on v0

--- a/solution.py
+++ b/solution.py
@@ -45,7 +45,9 @@
     scaled = local_float * inv_rms
     normed = (scaled * norm_gain).astype(jnp.bfloat16)
     group_rows = lax.all_gather(normed, "tensor", axis=0, tiled=True)
-    gathered = lax.all_gather(tile_values, "fsdp", axis=0, tiled=True)
+    gathered = jnp.concatenate(
+        lax.all_to_all(jnp.stack([tile_values] * lax.axis_size("fsdp")), "fsdp", 0, 0), axis=0
+    )
     kept_values = jnp.where(held_all[:, None, None], gathered, jnp.zeros_like(gathered))
     outputs = tile_forward(group_rows, kept_values, rows_list, cols_list, col_tiles)
     mixed = outputs.astype(jnp.bfloat16)

time: 849 us -> 727 us (0.86)
  waiting for transfers between devices: 639 us -> 498 us
  starting transfers between devices: 0.2 us -> 16.4 us
    all_gather x1 -> x0, waiting for transfers between devices: 208 us -> none  [per_device(): gathered = lax.all_gather(tile_values, 'fsdp', axis=0, tiled=True)]
    all_to_all x0 -> x1, waiting for transfers between devices: none -> 86.3 us  [per_device(): lax.all_to_all(jnp.stack([tile_values] * lax.axis_size('fsdp')), 'fsdp',...]
    reduce_scatter x1, waiting for transfers between devices: 163 us -> 145 us  [per_device(): lax.psum_scatter(tile_backward(grad_out, kept_values, rows_list, cols_lis...]
    all_to_all x0 -> x1, starting transfers between devices: none -> 16.2 us  [per_device(): lax.all_to_all(jnp.stack([tile_values] * lax.axis_size('fsdp')), 'fsdp',...]
  transfers between devices with their start and end apart: 5 -> 5, of which waited for: 5 -> 5; matrix products, arithmetic and copies ran while one was open for 3% -> 4% of each run, Pallas kernels for 0% -> 0%
where the time goes in v1:
time: 727 us; the launch traced here: 726 us
  waiting for transfers between devices  498 us (69%)
  blocking collectives  103 us (14%)
  other arithmetic  40.6 us (6%)
  local copies, waits for them, and re-layouts  35.4 us (5%)
  matrix products  18.2 us (3%)
  starting transfers between devices  16.4 us (2%)
  between operations  14 us (2%)
    reduce_scatter x1, waiting for transfers between devices, per_device(): lax.psum_scatter(tile_backward(grad_out, kept_values, rows_list, cols_lis...  145 us
    reduce_scatter x1, waiting for transfers between devices, per_device(): lax.psum_scatter(jnp.einsum('tsk,tsn->skn', picked_x, picked_g, preferred...  121 us
    all_gather x1, waiting for transfers between devices, per_device(): group_rows = lax.all_gather(normed, 'tensor', axis=0, tiled=True)  110 us
    psum x1, blocking collectives, per_device(): grad_gain = lax.psum(gain_part, ('dp', 'fsdp', 'tensor'))  103 us
    all_to_all x1, waiting for transfers between devices, per_device(): lax.all_to_all(jnp.stack([tile_values] * lax.axis_size('fsdp')), 'fsdp',...  86.3 us
    psum x1, waiting for transfers between devices, per_device(): grad_tiles = lax.psum(grad_shard, 'dp')  36.2 us
    scatter-add x1, other arithmetic, tile_backward(): placed = jnp.zeros((grad_rows.shape[0], row_tiles, tile_size), jnp.float3...  19.4 us
    all_to_all x1, starting transfers between devices, per_device(): lax.all_to_all(jnp.stack([tile_values] * lax.axis_size('fsdp')), 'fsdp',...  16.2 us
  transfers between devices with their start and end apart: 5, of which 5 were waited for; matrix products, arithmetic and copies ran while one was open for 4% of the time, Pallas kernels for 0%

profile of v1, /device:TPU:1, one launch (start us, length us, event | category | flops | bytes accessed | tf_op | source)
XLA Modules:
  0.0 726.1 jit_solution(1442723272345168450)
XLA Ops:
  7.2 2.8 stack.2
  10.0 16.2 %all-to-all-start = ((bf16[32,2,128,128]{3,2,1,0:T(8,128)(2,1)}), bf16[32,2,128,128]{3,2,1,0:T(8,128)(2,1)S(1)}, u32[]{:S(2)}, u32[]{:S(2)}) async-start(bf16[32,2,128,128]{3,2,1,0:T(8,128)(2,1)} %stack.2), calls=%async_computation | async-start | bytes 4194304 | tf_op jit(solution)/shard_map/all_to_all | solution.py:49
  29.3 3.1 gather_fusion.1
  32.4 86.3 %all-to-all-done = bf16[32,2,128,128]{3,2,1,0:T(8,128)(2,1)S(1)} async-done(((bf16[32,2,128,128]{3,2,1,0:T(8,128)(2,1)}), bf16[32,2,128,128]{3,2,1,0:T(8,128)(2,1)S(1)}, u32[]{:S(2)}, u32[]{:S(2)}) %all-to-all-start) | async-done | bytes 2097184 | tf_op jit(solution)/shard_map/all_to_all | solution.py:49
  119.1 2.6 copy-done.2
  121.7 4.5 fusion.2
  126.2 2.4 broadcast_in_dim.57
  128.7 19.4 %scatter_fusion.1 = f32[256,32,128]{2,0,1:T(8,128)} fusion(f32[256,32,128]{2,0,1:T(8,128)} %broadcast_in_dim.57, s32[64]{0:T(128)S(1)} %fusion.18, f32[64,256,128]{2,1,0:T(8,128)} %fusion.2), kind=kCustom, calls=%fused_computation.3 | custom fusion | flops 2097152 | bytes 25166080 | tf_op jit(solution)/shard_map/scatter-add | solution.py:28
  148.0 2.5 convert_element_type.28
  150.6 2.9 copy.34
  153.5 4.1 copy.39
  157.9 144.6 %reduce-scatter.7.cloned.1.call-done = bf16[32,4096]{1,0:T(8,128)(2,1)} async-done(((bf16[256,4096]{1,0:T(8,128)(2,1)}), bf16[32,4096]{1,0:T(8,128)(2,1)}) %reduce-scatter.7.cloned.1.call-update) | async-done | bytes 262160 | tf_op jit(solution)/shard_map/reduce_scatter | solution.py:54
  303.8 1.9 fusion.12
  305.8 110.0 %all-gather.2.cloned.1.call-done = bf16[256,4096]{1,0:T(8,128)(2,1)} async-done(((bf16[32,4096]{1,0:T(8,128)(2,1)}), bf16[256,4096]{1,0:T(8,128)(2,1)}) %all-gather.2.cloned.1.call-update) | async-done | bytes 2097168 | tf_op jit(solution)/shard_map/all_gather | solution.py:47
  415.8 4.1 copy.29
  419.8 3.2 copy.30
  423.1 3.0 gather_fusion
  426.1 7.0 fusion
  434.4 103.1 %psum.14 = f32[4096]{0:T(1024)} all-reduce(f32[4096]{0:T(1024)S(1)} %get-tuple-element.18), channel_id=1, replica_groups=mesh['dp'=2,'fsdp'=32,'tensor'=8] {'dp','fsdp','tensor'}, use_global_device_ids=true, to_apply=%region_6.9 | all-reduce | flops 4096 | bytes 32768 | tf_op jit(solution)/shard_map/psum | solution.py:73
  537.5 121.2 %reduce-scatter.5.cloned.1.call-done = f32[2,128,128]{2,1,0:T(8,128)} async-done(((f32[64,128,128]{2,1,0:T(8,128)}), f32[2,128,128]{2,1,0:T(8,128)}) %reduce-scatter.5.cloned.1.call-update) | async-done | bytes 131088 | tf_op jit(solution)/shard_map/reduce_scatter | solution.py:64
  658.7 1.6 broadcast_select_fusion.6
  660.4 6.7 fusion.5
  667.3 12.4 %scatter_fusion = f32[256,14,128]{2,0,1:T(8,128)S(1)} fusion(f32[256,14,128]{2,0,1:T(8,128)S(1)} %broadcast_in_dim.54, s32[64]{0:T(128)S(1)} %fusion.17, f32[64,256,128]{2,1,0:T(8,128)} %fusion.5), kind=kCustom, calls=%fused_computation.2 | custom fusion | flops 2097152 | bytes 25166080 | tf_op jit(solution)/shard_map/scatter-add | solution.py:15
  681.8 36.2 %all-reduce.2.cloned.1.call-done = f32[2,128,128]{2,1,0:T(8,128)} async-done(((f32[2,128,128]{2,1,0:T(8,128)}), f32[2,128,128]{2,1,0:T(8,128)}) %all-reduce.2.cloned.1.call-update) | async-done | bytes 131088 | tf_op jit(solution)/shard_map/psum | solution.py:71
  (48 shorter events, 10.2 us)
Async XLA Ops:
  7.2 19.1 %copy-start.4 = (bf16[256,1792]{1,0:T(8,128)(2,1)S(1)}, bf16[256,1792]{1,0:T(8,128)(2,1)}, u32[]{:S(2)}) copy-start(bf16[256,1792]{1,0:T(8,128)(2,1)} %param.17) | copy-start | bytes 2752516
  10.0 19.1 %copy-start.6 = (s32[1,32]{1,0:T(1,128)S(1)}, s32[1,32]{1,0:T(1,128)}, u32[]{:S(2)}) copy-start(s32[1,32]{1,0:T(1,128)} %param.16) | copy-start | bytes 388
  10.0 19.3 %copy-start.8 = (s32[1,64]{1,0:T(1,128)S(1)}, s32[1,64]{1,0:T(1,128)}, u32[]{:S(2)}) copy-start(s32[1,64]{1,0:T(1,128)} %param.15) | copy-start | bytes 772
  10.0 108.8 %all-to-all-start = ((bf16[32,2,128,128]{3,2,1,0:T(8,128)(2,1)}), bf16[32,2,128,128]{3,2,1,0:T(8,128)(2,1)S(1)}, u32[]{:S(2)}, u32[]{:S(2)}) async-start(bf16[32,2,128,128]{3,2,1,0:T(8,128)(2,1)} %stack.2), calls=%async_computation | async-start | bytes 4194304 | tf_op jit(solution)/shard_map/all_to_all | solution.py:49
  26.2 276.3 %reduce-scatter.7.cloned.1.call-start = ((), (), s32[]{:S(2)}) async-start(), calls=%async_computation.6 | async-start | bytes 2359296 | tf_op jit(solution)/shard_map/reduce_scatter | solution.py:54
  29.3 3.1 copy-start.7
  118.8 2.9 copy-start.2
  119.1 7.1 copy-start
  153.5 4.2 copy-start.3
  153.5 149.0 %copy-start.5 = (f32[4096]{0:T(1024)S(1)}, f32[4096]{0:T(1024)}, u32[]{:S(2)}) copy-start(f32[4096]{0:T(1024)} %param.12) | copy-start | bytes 49156
  157.7 258.1 %all-gather.2.cloned.1.call-start = ((), (), s32[]{:S(2)}) async-start(), calls=%async_computation.3 | async-start | bytes 2359296 | tf_op jit(solution)/shard_map/all_gather | solution.py:47
  305.7 353.0 %reduce-scatter.5.cloned.1.call-start = ((), (), s32[]{:S(2)}) async-start(), calls=%async_computation.4 | async-start | bytes 4325376 | tf_op jit(solution)/shard_map/reduce_scatter | solution.py:64
  433.1 227.3 %copy-start.1 = (bf16[64,128,128]{2,1,0:T(8,128)(2,1)S(1)}, bf16[64,128,128]{2,1,0:T(8,128)(2,1)}, u32[]{:S(2)}) copy-start(bf16[64,128,128]{2,1,0:T(8,128)(2,1)} %copy-done) | copy-start | bytes 6291460
  433.1 284.8 %all-reduce.2.cloned.1.call-start = ((), (), s32[]{:S(2)}) async-start(), calls=%async_computation.5 | async-start | bytes 262144 | tf_op jit(solution)/shard_map/psum | solution.py:71
Sparse Core Ops, SparseCore 0:
  157.8 144.6 reduce-scatter.6
  306.7 108.9 all-gather.1
  433.2 225.4 reduce-scatter.4
  662.3 55.6 all-reduce.1
